TPU v7x, 32 devices: a whole 2x2x4 slice. The times are simulated.
32 devices in a mesh: chan: 8 (over y, x, core), seg: 4 (over z).
Axes of the slice: x: 2, y: 2, z: 4, core: 2. Of those that a mesh axis runs over, the one named last changes fastest.
Arguments:
- spectra: bfloat16 [2, 32, 256, 512], P(None, 'seg', 'chan'), may hold values from -6 to 6
- sources: int32 [8, 4], replicated, may hold values from 0 to 255, as said below
Outputs:
- correlations: float32 [32, 256, 512], P(None, ('chan', 'seg'))
Inputs may be any that keep to these rules, and one draw needn't show every extreme that they name: `sources`: each entry names a channel of the array; entries may repeat and may crowd onto the channels of a few devices of chan.
All inputs are finite; a program needn't handle non-finite values.
Results may differ from a plain program's by a relative error of at most 0.004.
Values may be sent and summed in bfloat16 or wider, within the bound.
A program may use at most 128 MiB of HBM per device.

v0:
```python
import functools
import math

import jax
import jax.numpy as jnp
import ml_dtypes
import numpy as np
from jax import lax
from jax.experimental import pallas as pl
from jax.experimental.pallas import tpu as pltpu
from jax.sharding import PartitionSpec as P

LAGS = 256
MESH = pl.DeviceIdType.MESH


def whiten(spectra):
    values = spectra.astype(jnp.float32)
    power_mean = jnp.mean(values[0] * values[0] + values[1] * values[1], axis=-1)
    inv_scale = lax.rsqrt(power_mean + 1e-06)
    return (values * inv_scale[None, :, :, None]).astype(jnp.bfloat16)


def lag_matrix(freqs, half_lags):
    period = 2 * freqs
    rows = jnp.arange(freqs, dtype=jnp.int32)
    shifts = jnp.arange(2 * half_lags, dtype=jnp.int32) - half_lags
    phase = jnp.mod(rows[:, None] * shifts[None, :], period)
    angles = phase.astype(jnp.float32) * (2.0 * math.pi / period)
    return jnp.concatenate([jnp.cos(angles), -jnp.sin(angles)], axis=0)


def lag_halves(freqs, half_lags):
    period = 2 * freqs
    phase = np.mod(np.arange(freqs)[:, None] * (np.arange(2 * half_lags) - half_lags)[None, :], period)
    angles = phase * (2.0 * math.pi / period)
    table = np.concatenate([np.cos(angles), -np.sin(angles)], axis=0)
    high = table.astype(np.float32).astype(ml_dtypes.bfloat16)
    low = (table - high.astype(np.float64)).astype(np.float32).astype(ml_dtypes.bfloat16)
    return np.stack([high, low])


def correlate(source_spec, receiver_spec, lag_table):
    segs = receiver_spec.shape[1]
    freqs = receiver_spec.shape[3]
    real_part = jnp.einsum(
        "pkf,krf->prf", source_spec[0], receiver_spec[0], preferred_element_type=jnp.float32
    ) + jnp.einsum(
        "pkf,krf->prf", source_spec[1], receiver_spec[1], preferred_element_type=jnp.float32
    )
    imag_part = jnp.einsum(
        "pkf,krf->prf", source_spec[0], receiver_spec[1], preferred_element_type=jnp.float32
    ) - jnp.einsum(
        "pkf,krf->prf", source_spec[1], receiver_spec[0], preferred_element_type=jnp.float32
    )
    stacked = jnp.concatenate([real_part, imag_part], axis=-1) * (1.0 / math.sqrt(segs))
    flat = stacked.reshape(-1, 2 * freqs)
    result = jnp.dot(
        flat, lag_table, precision=lax.Precision.HIGHEST, preferred_element_type=jnp.float32
    ) * (1.0 / math.sqrt(freqs))
    return result.reshape(stacked.shape[0], stacked.shape[1], -1)


def shards(spectra, sources):
    whitened = whiten(spectra)
    regrouped = lax.all_to_all(whitened, "seg", split_axis=2, concat_axis=1, tiled=True)
    ch_dev = spectra.shape[2]
    freqs = spectra.shape[3]
    first_row = lax.axis_index("chan") * ch_dev
    lag_table = lag_matrix(freqs, LAGS)
    batches = sources.shape[0]
    results = []
    for batch_no in range(batches):
        local_row = sources[batch_no] - first_row
        onehot = (local_row[:, None] == jnp.arange(ch_dev, dtype=jnp.int32)[None, :]).astype(
            jnp.bfloat16
        )
        local_spec = lax.psum(
            jnp.einsum("pc,xscf->xpsf", onehot, whitened, preferred_element_type=jnp.float32),
            "chan",
        ).astype(jnp.bfloat16)
        source_spec = lax.all_gather(local_spec, "seg", axis=2, tiled=True)
        results.append(correlate(source_spec, regrouped, lag_table))
    return jnp.concatenate(results, axis=0)


CHANS = 8
CHIPS = 4
PLANES = 4


def kernel(spectra, sources, table, out, whs, sel, rs_in, rcv, src, vf, wf, acc, tab,
           rs_s, rs_r, a_s, a_r, z_s, z_r, c_s, c_r, p_s, p_r, t_sem):
    d = lax.axis_index("chan")
    z = lax.axis_index("seg")
    chip, core = d // 2, lax.rem(d, 2)
    segs, rows, freqs = spectra.shape[1:]
    n_src = out.shape[0]
    own = rows // PLANES
    tiles = freqs // 128

    table_in = pltpu.make_async_copy(table, tab, t_sem)
    table_in.start()

    def chan_at(o):
        return lax.rem(d + o, CHANS)

    def seg_at(o):
        return lax.rem(z + o, PLANES)

    def to(src_ref, dst_ref, s, r, where):
        return pltpu.make_async_remote_copy(
            src_ref=src_ref, dst_ref=dst_ref, send_sem=s, recv_sem=r,
            device_id=where, device_id_type=MESH)

    picks = {o: to(sel.at[chan_at(o)], rs_in.at[o], rs_s.at[o], rs_r.at[o], {"chan": chan_at(o)})
             for o in range(1, CHANS)}
    regroup = {o: to(whs.at[seg_at(o)], rcv.at[o], a_s.at[o], a_r.at[o], {"seg": seg_at(o)})
               for o in range(1, PLANES)}
    planes = {o: to(src.at[0, 0, 0], src.at[0, o, 0], z_s.at[o], z_r.at[o], {"seg": seg_at(o)})
              for o in range(1, PLANES)}
    chips = {(y, o): to(src.at[0, y, 0], src.at[0, y, o], c_s.at[y, o], c_r.at[y, o],
                        {"chan": lax.rem(chip + o, CHIPS) * 2 + core})
             for y in range(PLANES) for o in range(1, CHIPS)}
    cores = {(y, o): to(src.at[0, y, o], src.at[1, y, o], p_s.at[y, o], p_r.at[y, o],
                        {"chan": d + 1 - 2 * core})
             for y in range(PLANES) for o in range(CHIPS)}

    barrier = pltpu.get_barrier_semaphore()
    for o in range(1, CHANS):
        pl.semaphore_signal(barrier, inc=1, device_id={"chan": chan_at(o)}, device_id_type=MESH)
    for o in range(1, PLANES):
        pl.semaphore_signal(barrier, inc=1, device_id={"seg": seg_at(o)}, device_id_type=MESH)

    row = lax.broadcasted_iota(jnp.int32, (n_src, rows), 0)
    named = jnp.zeros((n_src, rows), jnp.int32)
    per = sources.shape[1]
    for n in range(n_src):
        named = jnp.where(row == n, sources[n // per, n % per], named)
    held = lax.broadcasted_iota(jnp.int32, (n_src, rows), 1) + d * rows
    onehot = (named == held).astype(jnp.float32).astype(jnp.bfloat16)

    def prepare(k):
        re = spectra[0, k].astype(jnp.float32)
        im = spectra[1, k].astype(jnp.float32)
        inv = lax.rsqrt(jnp.mean(re * re + im * im, axis=-1, keepdims=True) + 1e-06)
        re = (re * inv).astype(jnp.bfloat16)
        im = (im * inv).astype(jnp.bfloat16)
        for c, part in enumerate((re, im)):
            sel[k, c] = jnp.dot(onehot, part, preferred_element_type=jnp.float32).astype(jnp.bfloat16)
        re, im = re.astype(jnp.float32), im.astype(jnp.float32)
        for q in range(PLANES):
            cut = slice(q * own, (q + 1) * own)
            whs[q, k] = jnp.concatenate([re[cut], im[cut]], axis=0).astype(jnp.bfloat16)

    prepare(chan_at(1))
    pl.semaphore_wait(barrier, CHANS - 1 + PLANES - 1)
    picks[1].start()
    for o in range(2, CHANS):
        prepare(chan_at(o))
        picks[o].start()
    prepare(d)
    for o in range(1, PLANES):
        regroup[o].start()

    total = sel[d].astype(jnp.float32)
    for o in range(1, CHANS):
        picks[o].wait_recv()
        total = total + rs_in[o].astype(jnp.float32)
    src[0, 0, 0] = total.astype(jnp.bfloat16)
    for o in range(1, PLANES):
        planes[o].start()
    for o in range(1, CHIPS):
        chips[0, o].start()
    cores[0, 0].start()

    def receivers(y):
        for k in range(segs):
            wf[y, k] = (whs[z, k] if y == 0 else rcv[y, k]).astype(jnp.float32)

    def add(y, s, first):
        side = core if s == 0 else 1 - core
        ks = []
        for o in range(CHIPS):
            vf[o] = src[s, y, o].astype(jnp.float32)
            ks.append(lax.rem(chip - o + CHIPS, CHIPS) * 2 + side)
        for t in range(tiles):
            f = slice(t * 128, (t + 1) * 128)
            g = slice(freqs + t * 128, freqs + (t + 1) * 128)
            c = [wf[y, k, 0:own, f] for k in ks]
            e = [wf[y, k, own:2 * own, f] for k in ks]

            def some(m, carry):
                at = pl.ds(pl.multiple_of(m * 8, 8), 8)
                a8 = [vf[o, 0, at, f] for o in range(CHIPS)]
                b8 = [vf[o, 1, at, f] for o in range(CHIPS)]
                for j in range(8):
                    n = m * 8 + j
                    re = im = None
                    for o in range(CHIPS):
                        a = jnp.broadcast_to(a8[o][j:j + 1], (own, 128))
                        b = jnp.broadcast_to(b8[o][j:j + 1], (own, 128))
                        r, i = a * c[o] + b * e[o], a * e[o] - b * c[o]
                        re, im = (r, i) if o == 0 else (re + r, im + i)
                    if not first:
                        re, im = acc[n, :, f] + re, acc[n, :, g] + im
                    acc[n, :, f] = re
                    acc[n, :, g] = im
                return carry

            lax.fori_loop(0, n_src // 8, some, 0)

    receivers(0)
    for o in range(1, CHIPS):
        chips[0, o].wait_recv()
        cores[0, o].start()
    add(0, 0, True)
    for y in range(1, PLANES):
        planes[y].wait_recv()
        for o in range(1, CHIPS):
            chips[y, o].start()
        cores[y, 0].start()
    for o in range(CHIPS):
        cores[0, o].wait_recv()
    add(0, 1, False)
    for y in range(1, PLANES):
        for o in range(1, CHIPS):
            chips[y, o].wait_recv()
            cores[y, o].start()
        regroup[y].wait_recv()
        receivers(y)
        add(y, 0, False)
        for o in range(CHIPS):
            cores[y, o].wait_recv()
        add(y, 1, False)

    table_in.wait()
    scale = 1.0 / math.sqrt(segs * PLANES) / math.sqrt(freqs)
    step = 8

    def lags(m, carry):
        part = acc[pl.ds(m * step, step)].reshape(step * own, 2 * freqs)
        high = part.astype(jnp.bfloat16)
        low = (part - high.astype(jnp.float32)).astype(jnp.bfloat16)
        dot = functools.partial(jnp.dot, preferred_element_type=jnp.float32)
        result = dot(high, tab[0]) + (dot(low, tab[0]) + dot(high, tab[1]))
        out[pl.ds(m * step, step)] = (result * scale).reshape(step, own, -1)
        return carry

    lax.fori_loop(0, n_src // step, lags, 0)

    for group in (picks, regroup, planes, chips, cores):
        for copy in group.values():
            copy.wait_send()


def fused(spectra, sources):
    _, segs, rows, freqs = spectra.shape
    n_src = sources.shape[0] * sources.shape[1]
    own = rows // PLANES
    bf16, f32 = jnp.bfloat16, jnp.float32
    dma = pltpu.SemaphoreType.DMA
    return pl.pallas_call(
        kernel,
        out_shape=jax.ShapeDtypeStruct((n_src, own, 2 * LAGS), f32),
        in_specs=[
            pl.BlockSpec(memory_space=pltpu.VMEM),
            pl.BlockSpec(memory_space=pltpu.SMEM),
            pl.BlockSpec(memory_space=pl.ANY),
        ],
        out_specs=pl.BlockSpec(memory_space=pltpu.VMEM),
        scratch_shapes=[
            pltpu.VMEM((PLANES, segs, 2 * own, freqs), bf16),
            pltpu.VMEM((segs, 2, n_src, freqs), bf16),
            pltpu.VMEM((CHANS, 2, n_src, freqs), bf16),
            pltpu.VMEM((PLANES, segs, 2 * own, freqs), bf16),
            pltpu.VMEM((2, PLANES, CHIPS, 2, n_src, freqs), bf16),
            pltpu.VMEM((CHIPS, 2, n_src, freqs), f32),
            pltpu.VMEM((PLANES, segs, 2 * own, freqs), f32),
            pltpu.VMEM((n_src, own, 2 * freqs), f32),
            pltpu.VMEM((2, 2 * freqs, 2 * LAGS), bf16),
            dma((CHANS,)), dma((CHANS,)),
            dma((PLANES,)), dma((PLANES,)),
            dma((PLANES,)), dma((PLANES,)),
            dma((PLANES, CHIPS)), dma((PLANES, CHIPS)),
            dma((PLANES, CHIPS)), dma((PLANES, CHIPS)),
            dma,
        ],
        compiler_params=pltpu.CompilerParams(
            collective_id=0, has_side_effects=True, vmem_limit_bytes=40 * 1024 * 1024),
    )(spectra, sources, jnp.asarray(lag_halves(freqs, LAGS)))


def solution(mesh):
    placed = (P(None, "seg", "chan", None), P())
    fits = mesh.shape["chan"] == CHANS and mesh.shape["seg"] == PLANES
    return jax.shard_map(
        fused if fits else shards,
        mesh=mesh,
        in_specs=placed,
        out_specs=P(None, ("chan", "seg"), None),
        check_vma=False,
    )
```

profile of v0, /device:TPU:0, one launch (start us, length us, event | category | flops | bytes accessed | tf_op | source)
XLA Modules:
  0.0 42.0 jit_solution(3911855058236552598)
XLA Ops:
  0.0 0.8 %copy.4.sources = s32[8,4]{1,0:T(8,128)S(1)} copy(s32[8,4]{0,1:T(4,128)} %param.4) | data formatting | bytes 256 | tf_op args[1]
  0.8 0.0 copy-start
  0.8 1.6 %copy-done = bf16[2,1024,512]{2,1,0:T(8,128)(2,1)S(1)} copy-done((bf16[2,1024,512]{2,1,0:T(8,128)(2,1)S(1)}, bf16[2,1024,512]{2,1,0:T(8,128)(2,1)}, u32[]{:S(2)}) %copy-start) | copy-done | bytes 2097176
  2.3 0.0 copy-start.1
  2.4 1.0 %copy-done.1 = bf16[2,8,32,512]{3,2,1,0:T(8,128)(2,1)S(1)} copy-done((bf16[2,8,32,512]{3,2,1,0:T(8,128)(2,1)S(1)}, bf16[2,8,32,512]{3,2,1,0:T(8,128)(2,1)}, u32[]{:S(2)}) %copy-start.1) | copy-done | bytes 524312
  3.4 37.8 %shard_map.37 = f32[32,8,512]{2,1,0:T(8,128)S(1)} custom-call(bf16[2,8,32,512]{3,2,1,0:T(8,128)(2,1)S(1)} %copy-done.1, s32[8,4]{1,0:T(8,128)S(1)} %copy.4.sources, bf16[2,1024,512]{2,1,0:T(8,128)(2,1)S(1)} %copy-done), custom_call_target="tpu_custom_call" | custom-call | tf_op jit(solution)/shard_map/pallas_call | solution.py:263
  41.2 0.8 %copy.6 = f32[32,8,512]{2,1,0:T(8,128)} copy(f32[32,8,512]{2,1,0:T(8,128)S(1)} %shard_map.37) | data formatting | bytes 1048576
Async XLA Ops:
  0.8 1.6 %copy-start = (bf16[2,1024,512]{2,1,0:T(8,128)(2,1)S(1)}, bf16[2,1024,512]{2,1,0:T(8,128)(2,1)}, u32[]{:S(2)}) copy-start(bf16[2,1024,512]{2,1,0:T(8,128)(2,1)} %constant.2.clone.table) | copy-start | bytes 6291460
  2.3 1.0 %copy-start.1 = (bf16[2,8,32,512]{3,2,1,0:T(8,128)(2,1)S(1)}, bf16[2,8,32,512]{3,2,1,0:T(8,128)(2,1)}, u32[]{:S(2)}) copy-start(bf16[2,8,32,512]{3,2,1,0:T(8,128)(2,1)} %spectra.1) | copy-start | bytes 1572868
where the time goes:
time: 42.2 us; the launch traced here: 42 us
  Pallas kernels  37.8 us (90%)
  local copies, waits for them, and re-layouts  4.18 us (10%)
    pallas_call x1, Pallas kernels, fused(): pl.pallas_call(kernel, out_shape=jax.ShapeDtypeStruct((n_src, own, 2 * LA...  37.8 us
    unnamed x6, local copies, waits for them, and re-layouts  4.18 us

commit v1 on v0

--- a/solution.py
+++ b/solution.py
@@ -89,21 +89,24 @@
 PLANES = 4
 
 
-def kernel(spectra, sources, table, out, whs, sel, rs_in, rcv, src, vf, wf, acc, tab,
-           rs_s, rs_r, a_s, a_r, z_s, z_r, c_s, c_r, p_s, p_r, t_sem):
+def kernel(spectra, sources, table, out, spec, whs, sel, core_in, rs_in, rcv, src, vf, wf, acc, tab,
+           i_sem, h_s, h_r, rs_s, rs_r, a_s, a_r, z_s, z_r, c_s, c_r, p_s, p_r, t_sem):
     d = lax.axis_index("chan")
     z = lax.axis_index("seg")
     chip, core = d // 2, lax.rem(d, 2)
-    segs, rows, freqs = spectra.shape[1:]
+    segs, rows, freqs = spec.shape[1:]
     n_src = out.shape[0]
     own = rows // PLANES
+    half = segs // 2
     tiles = freqs // 128
 
+    spectra_in = pltpu.make_async_copy(spectra, spec, i_sem)
+    spectra_in.start()
     table_in = pltpu.make_async_copy(table, tab, t_sem)
     table_in.start()
 
-    def chan_at(o):
-        return lax.rem(d + o, CHANS)
+    def chip_at(o):
+        return lax.rem(chip + o, CHIPS)
 
     def seg_at(o):
         return lax.rem(z + o, PLANES)
@@ -113,77 +116,139 @@
             src_ref=src_ref, dst_ref=dst_ref, send_sem=s, recv_sem=r,
             device_id=where, device_id_type=MESH)
 
-    picks = {o: to(sel.at[chan_at(o)], rs_in.at[o], rs_s.at[o], rs_r.at[o], {"chan": chan_at(o)})
-             for o in range(1, CHANS)}
-    regroup = {o: to(whs.at[seg_at(o)], rcv.at[o], a_s.at[o], a_r.at[o], {"seg": seg_at(o)})
-               for o in range(1, PLANES)}
-    planes = {o: to(src.at[0, 0, 0], src.at[0, o, 0], z_s.at[o], z_r.at[o], {"seg": seg_at(o)})
-              for o in range(1, PLANES)}
-    chips = {(y, o): to(src.at[0, y, 0], src.at[0, y, o], c_s.at[y, o], c_r.at[y, o],
-                        {"chan": lax.rem(chip + o, CHIPS) * 2 + core})
-             for y in range(PLANES) for o in range(1, CHIPS)}
-    cores = {(y, o): to(src.at[0, y, o], src.at[1, y, o], p_s.at[y, o], p_r.at[y, o],
-                        {"chan": d + 1 - 2 * core})
-             for y in range(PLANES) for o in range(CHIPS)}
+    partner = {"chan": d + 1 - 2 * core}
+
+    def mate(o):
+        return {"chan": chip_at(o) * 2 + core}
+
+    halves = [to(sel.at[1, o], core_in.at[o], h_s.at[o], h_r.at[o], partner) for o in range(CHIPS)]
+    picks = {o: to(sel.at[0, o], rs_in.at[o], rs_s.at[o], rs_r.at[o], mate(o)) for o in range(1, CHIPS)}
+    regroup = {(o, h): to(whs.at[seg_at(o), pl.ds(h * half, half)], rcv.at[o, pl.ds(h * half, half)],
+                          a_s.at[o, h], a_r.at[o, h], {"seg": seg_at(o)})
+               for o in range(1, PLANES) for h in range(2)}
+
+    def chips(y, o):
+        return to(src.at[0, y, 0], src.at[0, y, o], c_s.at[y, o], c_r.at[y, o], mate(o))
+
+    def cores(y, o):
+        return to(src.at[0, y, o], src.at[1, y, o], p_s.at[y, o], p_r.at[y, o], partner)
+
+    def right(y):
+        return to(src.at[0, y, 0], src.at[0, y + 1, 0], z_s.at[0, y], z_r.at[y + 1], {"seg": z + 1})
+
+    def left(y):
+        there = lax.rem(y + PLANES - 1, PLANES)
+        return to(src.at[0, y, 0], src.at[0, there, 0], z_s.at[1, y], z_r.at[there], {"seg": z - 1})
+
+    def relay(y, act):
+        from_left = z >= y
+
+        @pl.when(jnp.logical_and(from_left, z < PLANES - 1))
+        def _():
+            act(right(y))
+
+        from_right = jnp.logical_or(z < y, y == 0)
+
+        @pl.when(jnp.logical_and(from_right, z > 0))
+        def _():
+            act(left(y))
+
+    first, last = (PLANES - 1 - z) // (PLANES - 1), z // (PLANES - 1)
+    y1 = 1 + 2 * first
+    y3 = 2 - first + last
+    y2 = 6 - y1 - y3
 
     barrier = pltpu.get_barrier_semaphore()
-    for o in range(1, CHANS):
-        pl.semaphore_signal(barrier, inc=1, device_id={"chan": chan_at(o)}, device_id_type=MESH)
+    pl.semaphore_signal(barrier, inc=1, device_id=partner, device_id_type=MESH)
+    for o in range(1, CHIPS):
+        pl.semaphore_signal(barrier, inc=1, device_id=mate(o), device_id_type=MESH)
     for o in range(1, PLANES):
         pl.semaphore_signal(barrier, inc=1, device_id={"seg": seg_at(o)}, device_id_type=MESH)
 
     row = lax.broadcasted_iota(jnp.int32, (n_src, rows), 0)
     named = jnp.zeros((n_src, rows), jnp.int32)
-    per = sources.shape[1]
+    per = sources.shape[0]
     for n in range(n_src):
-        named = jnp.where(row == n, sources[n // per, n % per], named)
+        named = jnp.where(row == n, sources[n % per, n // per], named)
     held = lax.broadcasted_iota(jnp.int32, (n_src, rows), 1) + d * rows
     onehot = (named == held).astype(jnp.float32).astype(jnp.bfloat16)
 
-    def prepare(k):
-        re = spectra[0, k].astype(jnp.float32)
-        im = spectra[1, k].astype(jnp.float32)
+    def prepare(side, o):
+        k = chip_at(o) * 2 + (core if side == 0 else 1 - core)
+        re = spec[0, k].astype(jnp.float32)
+        im = spec[1, k].astype(jnp.float32)
         inv = lax.rsqrt(jnp.mean(re * re + im * im, axis=-1, keepdims=True) + 1e-06)
         re = (re * inv).astype(jnp.bfloat16)
         im = (im * inv).astype(jnp.bfloat16)
         for c, part in enumerate((re, im)):
-            sel[k, c] = jnp.dot(onehot, part, preferred_element_type=jnp.float32).astype(jnp.bfloat16)
+            picked = jnp.dot(onehot, part, preferred_element_type=jnp.float32)
+            sel[side, o, c] = picked.astype(jnp.bfloat16)
         re, im = re.astype(jnp.float32), im.astype(jnp.float32)
         for q in range(PLANES):
             cut = slice(q * own, (q + 1) * own)
             whs[q, k] = jnp.concatenate([re[cut], im[cut]], axis=0).astype(jnp.bfloat16)
 
-    prepare(chan_at(1))
-    pl.semaphore_wait(barrier, CHANS - 1 + PLANES - 1)
-    picks[1].start()
-    for o in range(2, CHANS):
-        prepare(chan_at(o))
-        picks[o].start()
-    prepare(d)
+    spectra_in.wait()
+    order = (1, 2, 3, 0)
+    for o in order:
+        prepare(1, o)
+        if o == 1:
+            pl.semaphore_wait(barrier, CHIPS + PLANES - 1)
+        halves[o].start()
+    for o in order:
+        prepare(0, o)
     for o in range(1, PLANES):
-        regroup[o].start()
-
-    total = sel[d].astype(jnp.float32)
-    for o in range(1, CHANS):
+        regroup[o, 0].start()
+
+    for o in order:
+        halves[o].wait_recv()
+        sel[0, o] = (sel[0, o].astype(jnp.float32) + core_in[o].astype(jnp.float32)).astype(jnp.bfloat16)
+        if o != 0:
+            picks[o].start()
+    total = sel[0, 0].astype(jnp.float32)
+    for o in range(1, CHIPS):
         picks[o].wait_recv()
         total = total + rs_in[o].astype(jnp.float32)
     src[0, 0, 0] = total.astype(jnp.bfloat16)
-    for o in range(1, PLANES):
-        planes[o].start()
-    for o in range(1, CHIPS):
-        chips[0, o].start()
-    cores[0, 0].start()
+
+    def spread(y):
+        relay(y, lambda copy: copy.start())
+        for o in range(1, CHIPS):
+            chips(y, o).start()
+        cores(y, 0).start()
+
+    def spread_far(y):
+        pltpu.make_async_remote_copy(
+            src_ref=src.at[0, y, 0], dst_ref=src.at[0, y, 0], send_sem=z_s.at[0, y], recv_sem=z_r.at[y],
+            device_id={"seg": seg_at(1)}, device_id_type=MESH).wait_recv()
+        spread(y)
+
+    def share(y):
+        for o in range(1, CHIPS):
+            chips(y, o).wait_recv()
+            cores(y, o).start()
 
     def receivers(y):
         for k in range(segs):
-            wf[y, k] = (whs[z, k] if y == 0 else rcv[y, k]).astype(jnp.float32)
-
-    def add(y, s, first):
+            wf[y, k] = (whs[z, k] if type(y) is int else rcv[y, k]).astype(jnp.float32)
+
+    def await_receivers(y):
+        for h in range(2):
+            at = rcv.at[y, pl.ds(h * half, half)]
+            pltpu.make_async_remote_copy(
+                src_ref=at, dst_ref=at, send_sem=a_s.at[y, h], recv_sem=a_r.at[y, h],
+                device_id={"seg": seg_at(1)}, device_id_type=MESH).wait_recv()
+        receivers(y)
+
+    def add(y, s, begin=False):
+        if s == 1:
+            for o in range(CHIPS):
+                cores(y, o).wait_recv()
         side = core if s == 0 else 1 - core
         ks = []
         for o in range(CHIPS):
             vf[o] = src[s, y, o].astype(jnp.float32)
-            ks.append(lax.rem(chip - o + CHIPS, CHIPS) * 2 + side)
+            ks.append(chip_at(CHIPS - o) * 2 + side)
         for t in range(tiles):
             f = slice(t * 128, (t + 1) * 128)
             g = slice(freqs + t * 128, freqs + (t + 1) * 128)
@@ -202,7 +267,7 @@
                         b = jnp.broadcast_to(b8[o][j:j + 1], (own, 128))
                         r, i = a * c[o] + b * e[o], a * e[o] - b * c[o]
                         re, im = (r, i) if o == 0 else (re + r, im + i)
-                    if not first:
+                    if not begin:
                         re, im = acc[n, :, f] + re, acc[n, :, g] + im
                     acc[n, :, f] = re
                     acc[n, :, g] = im
@@ -210,48 +275,46 @@
 
             lax.fori_loop(0, n_src // 8, some, 0)
 
+    spread(0)
     receivers(0)
-    for o in range(1, CHIPS):
-        chips[0, o].wait_recv()
-        cores[0, o].start()
+    share(0)
+    spread_far(y1)
+    for o in range(1, PLANES):
+        regroup[o, 1].start()
     add(0, 0, True)
-    for y in range(1, PLANES):
-        planes[y].wait_recv()
-        for o in range(1, CHIPS):
-            chips[y, o].start()
-        cores[y, 0].start()
-    for o in range(CHIPS):
-        cores[0, o].wait_recv()
-    add(0, 1, False)
-    for y in range(1, PLANES):
-        for o in range(1, CHIPS):
-            chips[y, o].wait_recv()
-            cores[y, o].start()
-        regroup[y].wait_recv()
-        receivers(y)
-        add(y, 0, False)
-        for o in range(CHIPS):
-            cores[y, o].wait_recv()
-        add(y, 1, False)
+    spread_far(y2)
+    add(0, 1)
+    spread_far(y3)
+    share(y1)
+    await_receivers(y1)
+    add(y1, 0)
+    share(y2)
+    add(y1, 1)
+    await_receivers(y2)
+    add(y2, 0)
+    share(y3)
+    add(y2, 1)
+    await_receivers(y3)
+    add(y3, 0)
+    add(y3, 1)
 
     table_in.wait()
     scale = 1.0 / math.sqrt(segs * PLANES) / math.sqrt(freqs)
-    step = 8
-
-    def lags(m, carry):
-        part = acc[pl.ds(m * step, step)].reshape(step * own, 2 * freqs)
-        high = part.astype(jnp.bfloat16)
-        low = (part - high.astype(jnp.float32)).astype(jnp.bfloat16)
-        dot = functools.partial(jnp.dot, preferred_element_type=jnp.float32)
-        result = dot(high, tab[0]) + (dot(low, tab[0]) + dot(high, tab[1]))
-        out[pl.ds(m * step, step)] = (result * scale).reshape(step, own, -1)
-        return carry
-
-    lax.fori_loop(0, n_src // step, lags, 0)
-
-    for group in (picks, regroup, planes, chips, cores):
-        for copy in group.values():
-            copy.wait_send()
+    flat = acc[...].reshape(n_src * own, 2 * freqs)
+    high = flat.astype(jnp.bfloat16)
+    low = (flat - high.astype(jnp.float32)).astype(jnp.bfloat16)
+    dot = functools.partial(jnp.dot, preferred_element_type=jnp.float32)
+    result = dot(high, tab[0]) + (dot(low, tab[0]) + dot(high, tab[1]))
+    out[...] = (result * scale).reshape(out.shape)
+
+    for copy in (*halves, *picks.values(), *regroup.values()):
+        copy.wait_send()
+    for y in range(PLANES):
+        relay(y, lambda copy: copy.wait_send())
+        for o in range(CHIPS):
+            if o > 0:
+                chips(y, o).wait_send()
+            cores(y, o).wait_send()
 
 
 def fused(spectra, sources):
@@ -264,31 +327,35 @@
         kernel,
         out_shape=jax.ShapeDtypeStruct((n_src, own, 2 * LAGS), f32),
         in_specs=[
-            pl.BlockSpec(memory_space=pltpu.VMEM),
+            pl.BlockSpec(memory_space=pl.ANY),
             pl.BlockSpec(memory_space=pltpu.SMEM),
             pl.BlockSpec(memory_space=pl.ANY),
         ],
         out_specs=pl.BlockSpec(memory_space=pltpu.VMEM),
         scratch_shapes=[
+            pltpu.VMEM((2, segs, rows, freqs), bf16),
             pltpu.VMEM((PLANES, segs, 2 * own, freqs), bf16),
-            pltpu.VMEM((segs, 2, n_src, freqs), bf16),
-            pltpu.VMEM((CHANS, 2, n_src, freqs), bf16),
+            pltpu.VMEM((2, CHIPS, 2, n_src, freqs), bf16),
+            pltpu.VMEM((CHIPS, 2, n_src, freqs), bf16),
+            pltpu.VMEM((CHIPS, 2, n_src, freqs), bf16),
             pltpu.VMEM((PLANES, segs, 2 * own, freqs), bf16),
             pltpu.VMEM((2, PLANES, CHIPS, 2, n_src, freqs), bf16),
             pltpu.VMEM((CHIPS, 2, n_src, freqs), f32),
             pltpu.VMEM((PLANES, segs, 2 * own, freqs), f32),
             pltpu.VMEM((n_src, own, 2 * freqs), f32),
             pltpu.VMEM((2, 2 * freqs, 2 * LAGS), bf16),
-            dma((CHANS,)), dma((CHANS,)),
-            dma((PLANES,)), dma((PLANES,)),
-            dma((PLANES,)), dma((PLANES,)),
+            dma,
+            dma((CHIPS,)), dma((CHIPS,)),
+            dma((CHIPS,)), dma((CHIPS,)),
+            dma((PLANES, 2)), dma((PLANES, 2)),
+            dma((2, PLANES)), dma((PLANES,)),
             dma((PLANES, CHIPS)), dma((PLANES, CHIPS)),
             dma((PLANES, CHIPS)), dma((PLANES, CHIPS)),
             dma,
         ],
         compiler_params=pltpu.CompilerParams(
-            collective_id=0, has_side_effects=True, vmem_limit_bytes=40 * 1024 * 1024),
-    )(spectra, sources, jnp.asarray(lag_halves(freqs, LAGS)))
+            collective_id=0, has_side_effects=True, vmem_limit_bytes=60 * 1024 * 1024),
+    )(spectra, sources.T, jnp.asarray(lag_halves(freqs, LAGS)))
 
 
 def solution(mesh):

time: 42.2 us -> 39.6 us (0.938)
  local copies, waits for them, and re-layouts: 4.18 us -> 1.87 us
    unnamed x6 -> x1, local copies, waits for them, and re-layouts: 4.18 us -> 1.87 us
where the time goes in v1:
time: 39.6 us; the launch traced here: 39.4 us
  Pallas kernels  37.5 us (95%)
  local copies, waits for them, and re-layouts  1.87 us (5%)
    pallas_call x1, Pallas kernels, fused(): pl.pallas_call(kernel, out_shape=jax.ShapeDtypeStruct((n_src, own, 2 * LA...  37.5 us
    unnamed x1, local copies, waits for them, and re-layouts  1.87 us

profile of v1, /device:TPU:0, one launch (start us, length us, event | category | flops | bytes accessed | tf_op | source)
XLA Modules:
  0.0 39.4 jit_solution(12328371746874032987)
XLA Ops:
  0.0 37.5 %shard_map.37 = f32[32,8,512]{2,1,0:T(8,128)} custom-call(bf16[2,8,32,512]{3,2,1,0:T(8,128)(2,1)} %spectra.1, s32[4,8]{1,0:T(4,128)} %bitcast.1, bf16[2,1024,512]{2,1,0:T(8,128)(2,1)} %constant.2.clone.table), custom_call_target="tpu_custom_call" | custom-call | tf_op jit(solution)/shard_map/pallas_call | solution.py:326
  37.5 1.9 %copy.5 = f32[32,8,512]{2,1,0:T(8,128)} copy(f32[32,8,512]{2,1,0:T(8,128)} %shard_map.37) | data formatting | bytes 1048576

commit v2 on v1

--- a/solution.py
+++ b/solution.py
@@ -123,9 +123,10 @@
 
     halves = [to(sel.at[1, o], core_in.at[o], h_s.at[o], h_r.at[o], partner) for o in range(CHIPS)]
     picks = {o: to(sel.at[0, o], rs_in.at[o], rs_s.at[o], rs_r.at[o], mate(o)) for o in range(1, CHIPS)}
-    regroup = {(o, h): to(whs.at[seg_at(o), pl.ds(h * half, half)], rcv.at[o, pl.ds(h * half, half)],
-                          a_s.at[o, h], a_r.at[o, h], {"seg": seg_at(o)})
-               for o in range(1, PLANES) for h in range(2)}
+
+    def regroup(o, h):
+        part = pl.ds(h * half, half)
+        return to(whs.at[seg_at(o), part], rcv.at[o, part], a_s.at[o, h], a_r.at[o, h], {"seg": seg_at(o)})
 
     def chips(y, o):
         return to(src.at[0, y, 0], src.at[0, y, o], c_s.at[y, o], c_r.at[y, o], mate(o))
@@ -157,6 +158,9 @@
     y1 = 1 + 2 * first
     y3 = 2 - first + last
     y2 = 6 - y1 - y3
+    far = 2 + first - last
+    near = 1 + first + last
+    reach = (far, near, 6 - far - near)
 
     barrier = pltpu.get_barrier_semaphore()
     pl.semaphore_signal(barrier, inc=1, device_id=partner, device_id_type=MESH)
@@ -197,8 +201,8 @@
         halves[o].start()
     for o in order:
         prepare(0, o)
-    for o in range(1, PLANES):
-        regroup[o, 0].start()
+    for o in reach:
+        regroup(o, 0).start()
 
     for o in order:
         halves[o].wait_recv()
@@ -249,42 +253,40 @@
         for o in range(CHIPS):
             vf[o] = src[s, y, o].astype(jnp.float32)
             ks.append(chip_at(CHIPS - o) * 2 + side)
-        for t in range(tiles):
-            f = slice(t * 128, (t + 1) * 128)
-            g = slice(freqs + t * 128, freqs + (t + 1) * 128)
-            c = [wf[y, k, 0:own, f] for k in ks]
-            e = [wf[y, k, own:2 * own, f] for k in ks]
-
-            def some(m, carry):
-                at = pl.ds(pl.multiple_of(m * 8, 8), 8)
-                a8 = [vf[o, 0, at, f] for o in range(CHIPS)]
-                b8 = [vf[o, 1, at, f] for o in range(CHIPS)]
-                for j in range(8):
-                    n = m * 8 + j
+
+        def tile(t, carry):
+            f = pl.ds(pl.multiple_of(t * 128, 128), 128)
+            g = pl.ds(pl.multiple_of(freqs + t * 128, 128), 128)
+            cs = [wf[y, k, 0:own, f] for k in ks]
+            es = [wf[y, k, own:2 * own, f] for k in ks]
+            for r in range(own):
+                c = [jnp.broadcast_to(v[r:r + 1], (8, 128)) for v in cs]
+                e = [jnp.broadcast_to(v[r:r + 1], (8, 128)) for v in es]
+                for m in range(n_src // 8):
+                    n = slice(m * 8, m * 8 + 8)
                     re = im = None
                     for o in range(CHIPS):
-                        a = jnp.broadcast_to(a8[o][j:j + 1], (own, 128))
-                        b = jnp.broadcast_to(b8[o][j:j + 1], (own, 128))
-                        r, i = a * c[o] + b * e[o], a * e[o] - b * c[o]
-                        re, im = (r, i) if o == 0 else (re + r, im + i)
+                        a, b = vf[o, 0, n, f], vf[o, 1, n, f]
+                        u, v = a * c[o] + b * e[o], a * e[o] - b * c[o]
+                        re, im = (u, v) if o == 0 else (re + u, im + v)
                     if not begin:
-                        re, im = acc[n, :, f] + re, acc[n, :, g] + im
-                    acc[n, :, f] = re
-                    acc[n, :, g] = im
-                return carry
-
-            lax.fori_loop(0, n_src // 8, some, 0)
+                        re, im = acc[r, n, f] + re, acc[r, n, g] + im
+                    acc[r, n, f] = re
+                    acc[r, n, g] = im
+            return carry
+
+        lax.fori_loop(0, tiles, tile, 0)
 
     spread(0)
     receivers(0)
     share(0)
     spread_far(y1)
-    for o in range(1, PLANES):
-        regroup[o, 1].start()
+    spread_far(y2)
+    for o in reach:
+        regroup(o, 1).start()
     add(0, 0, True)
-    spread_far(y2)
+    spread_far(y3)
     add(0, 1)
-    spread_far(y3)
     share(y1)
     await_receivers(y1)
     add(y1, 0)
@@ -305,9 +307,11 @@
     low = (flat - high.astype(jnp.float32)).astype(jnp.bfloat16)
     dot = functools.partial(jnp.dot, preferred_element_type=jnp.float32)
     result = dot(high, tab[0]) + (dot(low, tab[0]) + dot(high, tab[1]))
-    out[...] = (result * scale).reshape(out.shape)
-
-    for copy in (*halves, *picks.values(), *regroup.values()):
+    result = result * scale
+    for r in range(own):
+        out[:, r, :] = result[r * n_src:(r + 1) * n_src]
+
+    for copy in (*halves, *picks.values(), *(regroup(o, h) for o in range(1, PLANES) for h in range(2))):
         copy.wait_send()
     for y in range(PLANES):
         relay(y, lambda copy: copy.wait_send())
@@ -327,9 +331,9 @@
         kernel,
         out_shape=jax.ShapeDtypeStruct((n_src, own, 2 * LAGS), f32),
         in_specs=[
-            pl.BlockSpec(memory_space=pl.ANY),
+            pl.BlockSpec(memory_space=pltpu.HBM),
             pl.BlockSpec(memory_space=pltpu.SMEM),
-            pl.BlockSpec(memory_space=pl.ANY),
+            pl.BlockSpec(memory_space=pltpu.HBM),
         ],
         out_specs=pl.BlockSpec(memory_space=pltpu.VMEM),
         scratch_shapes=[
@@ -342,7 +346,7 @@
             pltpu.VMEM((2, PLANES, CHIPS, 2, n_src, freqs), bf16),
             pltpu.VMEM((CHIPS, 2, n_src, freqs), f32),
             pltpu.VMEM((PLANES, segs, 2 * own, freqs), f32),
-            pltpu.VMEM((n_src, own, 2 * freqs), f32),
+            pltpu.VMEM((own, n_src, 2 * freqs), f32),
             pltpu.VMEM((2, 2 * freqs, 2 * LAGS), bf16),
             dma,
             dma((CHIPS,)), dma((CHIPS,)),
@@ -354,7 +358,7 @@
             dma,
         ],
         compiler_params=pltpu.CompilerParams(
-            collective_id=0, has_side_effects=True, vmem_limit_bytes=60 * 1024 * 1024),
+            collective_id=0, has_side_effects=True, vmem_limit_bytes=40 * 1024 * 1024),
     )(spectra, sources.T, jnp.asarray(lag_halves(freqs, LAGS)))
 
 

time: 39.6 us -> 37.6 us (0.949)
  Pallas kernels: 37.5 us -> 33.2 us
  local copies, waits for them, and re-layouts: 1.87 us -> 4.11 us
    pallas_call x1, Pallas kernels: 37.5 us -> 33.2 us  [fused(): pl.pallas_call(kernel, out_shape=jax.ShapeDtypeStruct((n_src, own, 2 * LA...]
    unnamed x1 -> x7, local copies, waits for them, and re-layouts: 1.87 us -> 4.11 us
where the time goes in v2:
time: 37.6 us; the launch traced here: 37.4 us
  Pallas kernels  33.2 us (88%)
  local copies, waits for them, and re-layouts  4.11 us (11%)
    pallas_call x1, Pallas kernels, fused(): pl.pallas_call(kernel, out_shape=jax.ShapeDtypeStruct((n_src, own, 2 * LA...  33.2 us
    unnamed x7, local copies, waits for them, and re-layouts  4.11 us

profile of v2, /device:TPU:0, one launch (start us, length us, event | category | flops | bytes accessed | tf_op | source)
XLA Modules:
  0.0 37.4 jit_solution(975806499303016449)
XLA Ops:
  0.0 0.0 copy-start
  0.0 1.6 %copy-done = bf16[2,1024,512]{2,1,0:T(8,128)(2,1)S(1)} copy-done((bf16[2,1024,512]{2,1,0:T(8,128)(2,1)S(1)}, bf16[2,1024,512]{2,1,0:T(8,128)(2,1)}, u32[]{:S(2)}) %copy-start) | copy-done | bytes 2097176
  1.6 0.0 copy-start.1
  1.6 1.0 %copy-done.1 = bf16[2,8,32,512]{3,2,1,0:T(8,128)(2,1)S(1)} copy-done((bf16[2,8,32,512]{3,2,1,0:T(8,128)(2,1)S(1)}, bf16[2,8,32,512]{3,2,1,0:T(8,128)(2,1)}, u32[]{:S(2)}) %copy-start.1) | copy-done | bytes 524312
  2.6 0.0 copy-start.2
  2.6 0.7 %copy-done.2 = s32[8,4]{0,1:T(4,128)S(1)} copy-done((s32[8,4]{0,1:T(4,128)S(1)}, s32[8,4]{0,1:T(4,128)}, u32[]{:S(2)}) %copy-start.2) | copy-done | bytes 152
  3.3 33.2 %shard_map.37 = f32[32,8,512]{2,1,0:T(8,128)S(1)} custom-call(bf16[2,8,32,512]{3,2,1,0:T(8,128)(2,1)S(1)} %copy-done.1, s32[4,8]{1,0:T(4,128)S(1)} %bitcast.1, bf16[2,1024,512]{2,1,0:T(8,128)(2,1)S(1)} %copy-done), custom_call_target="tpu_custom_call" | custom-call | tf_op jit(solution)/shard_map/pallas_call | solution.py:330
  36.6 0.8 %copy.5 = f32[32,8,512]{2,1,0:T(8,128)} copy(f32[32,8,512]{2,1,0:T(8,128)S(1)} %shard_map.37) | data formatting | bytes 1048576
Async XLA Ops:
  0.0 1.6 %copy-start = (bf16[2,1024,512]{2,1,0:T(8,128)(2,1)S(1)}, bf16[2,1024,512]{2,1,0:T(8,128)(2,1)}, u32[]{:S(2)}) copy-start(bf16[2,1024,512]{2,1,0:T(8,128)(2,1)} %constant.2.clone.table) | copy-start | bytes 6291460
  1.6 1.0 %copy-start.1 = (bf16[2,8,32,512]{3,2,1,0:T(8,128)(2,1)S(1)}, bf16[2,8,32,512]{3,2,1,0:T(8,128)(2,1)}, u32[]{:S(2)}) copy-start(bf16[2,8,32,512]{3,2,1,0:T(8,128)(2,1)} %spectra.1) | copy-start | bytes 1572868
  2.6 0.7 %copy-start.2 = (s32[8,4]{0,1:T(4,128)S(1)}, s32[8,4]{0,1:T(4,128)}, u32[]{:S(2)}) copy-start(s32[8,4]{0,1:T(4,128)} %param.4) | copy-start | bytes 388

commit v3 on v2

--- a/solution.py
+++ b/solution.py
@@ -106,7 +106,8 @@
     table_in.start()
 
     def chip_at(o):
-        return lax.rem(chip + o, CHIPS)
+        x_too = 1 - 2 * lax.rem(chip, 2) if o % 2 else 0
+        return lax.rem(chip + x_too + (o // 2) * 2, CHIPS)
 
     def seg_at(o):
         return lax.rem(z + o, PLANES)
@@ -130,6 +131,10 @@
 
     def chips(y, o):
         return to(src.at[0, y, 0], src.at[0, y, o], c_s.at[y, o], c_r.at[y, o], mate(o))
+
+    def across(y, o):
+        c = o - 1
+        return to(src.at[0, y, o, c], src.at[0, y, 3, c], c_s.at[y, o + 2], c_r.at[y, o + 2], mate(3 - o))
 
     def cores(y, o):
         return to(src.at[0, y, o], src.at[1, y, o], p_s.at[y, o], p_r.at[y, o], partner)
@@ -217,7 +222,7 @@
 
     def spread(y):
         relay(y, lambda copy: copy.start())
-        for o in range(1, CHIPS):
+        for o in (1, 2):
             chips(y, o).start()
         cores(y, 0).start()
 
@@ -228,9 +233,15 @@
         spread(y)
 
     def share(y):
-        for o in range(1, CHIPS):
+        for o in (1, 2):
             chips(y, o).wait_recv()
+            across(y, o).start()
             cores(y, o).start()
+
+    def share_across(y):
+        for o in (1, 2):
+            across(y, o).wait_recv()
+        cores(y, 3).start()
 
     def receivers(y):
         for k in range(segs):
@@ -252,7 +263,7 @@
         ks = []
         for o in range(CHIPS):
             vf[o] = src[s, y, o].astype(jnp.float32)
-            ks.append(chip_at(CHIPS - o) * 2 + side)
+            ks.append(chip_at(o) * 2 + side)
 
         def tile(t, carry):
             f = pl.ds(pl.multiple_of(t * 128, 128), 128)
@@ -281,20 +292,24 @@
     receivers(0)
     share(0)
     spread_far(y1)
+    share_across(0)
     spread_far(y2)
     for o in reach:
         regroup(o, 1).start()
+    share(y1)
     add(0, 0, True)
     spread_far(y3)
+    share(y2)
+    share_across(y1)
     add(0, 1)
-    share(y1)
+    share(y3)
     await_receivers(y1)
     add(y1, 0)
-    share(y2)
+    share_across(y2)
     add(y1, 1)
+    share_across(y3)
     await_receivers(y2)
     add(y2, 0)
-    share(y3)
     add(y2, 1)
     await_receivers(y3)
     add(y3, 0)
@@ -316,8 +331,9 @@
     for y in range(PLANES):
         relay(y, lambda copy: copy.wait_send())
         for o in range(CHIPS):
-            if o > 0:
+            if o in (1, 2):
                 chips(y, o).wait_send()
+                across(y, o).wait_send()
             cores(y, o).wait_send()
 
 
@@ -353,12 +369,12 @@
             dma((CHIPS,)), dma((CHIPS,)),
             dma((PLANES, 2)), dma((PLANES, 2)),
             dma((2, PLANES)), dma((PLANES,)),
-            dma((PLANES, CHIPS)), dma((PLANES, CHIPS)),
+            dma((PLANES, 5)), dma((PLANES, 5)),
             dma((PLANES, CHIPS)), dma((PLANES, CHIPS)),
             dma,
         ],
         compiler_params=pltpu.CompilerParams(
-            collective_id=0, has_side_effects=True, vmem_limit_bytes=40 * 1024 * 1024),
+            collective_id=0, has_side_effects=True, vmem_limit_bytes=60 * 1024 * 1024),
     )(spectra, sources.T, jnp.asarray(lag_halves(freqs, LAGS)))
 
 

time: 37.6 us -> 40.8 us (1.085)
  Pallas kernels: 33.2 us -> 38.8 us
  local copies, waits for them, and re-layouts: 4.11 us -> 1.87 us
    pallas_call x1, Pallas kernels: 33.2 us -> 38.8 us  [fused(): pl.pallas_call(kernel, out_shape=jax.ShapeDtypeStruct((n_src, own, 2 * LA...]
    unnamed x7 -> x1, local copies, waits for them, and re-layouts: 4.11 us -> 1.87 us
where the time goes in v3:
time: 40.8 us; the launch traced here: 40.6 us
  Pallas kernels  38.8 us (95%)
  local copies, waits for them, and re-layouts  1.87 us (5%)
    pallas_call x1, Pallas kernels, fused(): pl.pallas_call(kernel, out_shape=jax.ShapeDtypeStruct((n_src, own, 2 * LA...  38.8 us
    unnamed x1, local copies, waits for them, and re-layouts  1.87 us

profile of v3, /device:TPU:0, one launch (start us, length us, event | category | flops | bytes accessed | tf_op | source)
XLA Modules:
  0.0 40.6 jit_solution(6499619745263000746)
XLA Ops:
  0.0 38.8 %shard_map.37 = f32[32,8,512]{2,1,0:T(8,128)} custom-call(bf16[2,8,32,512]{3,2,1,0:T(8,128)(2,1)} %spectra.1, s32[4,8]{1,0:T(4,128)} %bitcast.1, bf16[2,1024,512]{2,1,0:T(8,128)(2,1)} %constant.2.clone.table), custom_call_target="tpu_custom_call" | custom-call | tf_op jit(solution)/shard_map/pallas_call | solution.py:346
  38.8 1.9 %copy.5 = f32[32,8,512]{2,1,0:T(8,128)} copy(f32[32,8,512]{2,1,0:T(8,128)} %shard_map.37) | data formatting | bytes 1048576

commit v4 on v2

--- a/solution.py
+++ b/solution.py
@@ -94,19 +94,26 @@
     d = lax.axis_index("chan")
     z = lax.axis_index("seg")
     chip, core = d // 2, lax.rem(d, 2)
-    segs, rows, freqs = spec.shape[1:]
+    segs, rows, freqs = spectra.shape[1:]
     n_src = out.shape[0]
     own = rows // PLANES
-    half = segs // 2
     tiles = freqs // 128
 
-    spectra_in = pltpu.make_async_copy(spectra, spec, i_sem)
-    spectra_in.start()
+    def chip_at(o):
+        return lax.rem(chip + o, CHIPS)
+
+    def side_at(side):
+        return core if side == 0 else 1 - core
+
+    def segment(side, o):
+        k = chip_at(o) * 2 + side_at(side)
+        return pltpu.make_async_copy(spectra.at[:, k], spec.at[side, o], i_sem.at[side, o])
+
+    for side in (1, 0):
+        for o in range(CHIPS):
+            segment(side, o).start()
     table_in = pltpu.make_async_copy(table, tab, t_sem)
     table_in.start()
-
-    def chip_at(o):
-        return lax.rem(chip + o, CHIPS)
 
     def seg_at(o):
         return lax.rem(z + o, PLANES)
@@ -121,12 +128,11 @@
     def mate(o):
         return {"chan": chip_at(o) * 2 + core}
 
-    halves = [to(sel.at[1, o], core_in.at[o], h_s.at[o], h_r.at[o], partner) for o in range(CHIPS)]
+    halves = to(sel.at[1], core_in, h_s, h_r, partner)
     picks = {o: to(sel.at[0, o], rs_in.at[o], rs_s.at[o], rs_r.at[o], mate(o)) for o in range(1, CHIPS)}
 
     def regroup(o, h):
-        part = pl.ds(h * half, half)
-        return to(whs.at[seg_at(o), part], rcv.at[o, part], a_s.at[o, h], a_r.at[o, h], {"seg": seg_at(o)})
+        return to(whs.at[seg_at(o), 1 - h], rcv.at[o, 1 - h], a_s.at[o, h], a_r.at[o, h], {"seg": seg_at(o)})
 
     def chips(y, o):
         return to(src.at[0, y, 0], src.at[0, y, o], c_s.at[y, o], c_r.at[y, o], mate(o))
@@ -177,35 +183,33 @@
     held = lax.broadcasted_iota(jnp.int32, (n_src, rows), 1) + d * rows
     onehot = (named == held).astype(jnp.float32).astype(jnp.bfloat16)
 
-    def prepare(side, o):
-        k = chip_at(o) * 2 + (core if side == 0 else 1 - core)
-        re = spec[0, k].astype(jnp.float32)
-        im = spec[1, k].astype(jnp.float32)
-        inv = lax.rsqrt(jnp.mean(re * re + im * im, axis=-1, keepdims=True) + 1e-06)
-        re = (re * inv).astype(jnp.bfloat16)
-        im = (im * inv).astype(jnp.bfloat16)
-        for c, part in enumerate((re, im)):
-            picked = jnp.dot(onehot, part, preferred_element_type=jnp.float32)
-            sel[side, o, c] = picked.astype(jnp.bfloat16)
-        re, im = re.astype(jnp.float32), im.astype(jnp.float32)
-        for q in range(PLANES):
-            cut = slice(q * own, (q + 1) * own)
-            whs[q, k] = jnp.concatenate([re[cut], im[cut]], axis=0).astype(jnp.bfloat16)
-
-    spectra_in.wait()
-    order = (1, 2, 3, 0)
-    for o in order:
-        prepare(1, o)
-        if o == 1:
-            pl.semaphore_wait(barrier, CHIPS + PLANES - 1)
-        halves[o].start()
-    for o in order:
-        prepare(0, o)
+    def prepare(side):
+        for o in range(CHIPS):
+            segment(side, o).wait()
+        for o in range(CHIPS):
+            re = spec[side, o, 0].astype(jnp.float32)
+            im = spec[side, o, 1].astype(jnp.float32)
+            inv = lax.rsqrt(jnp.mean(re * re + im * im, axis=-1, keepdims=True) + 1e-06)
+            re = (re * inv).astype(jnp.bfloat16)
+            im = (im * inv).astype(jnp.bfloat16)
+            for c, part in enumerate((re, im)):
+                picked = jnp.dot(onehot, part, preferred_element_type=jnp.float32)
+                sel[side, o, c] = picked.astype(jnp.bfloat16)
+            re, im = re.astype(jnp.float32), im.astype(jnp.float32)
+            for q in range(PLANES):
+                cut = slice(q * own, (q + 1) * own)
+                both = jnp.concatenate([re[cut], im[cut]], axis=0)
+                whs[q, side, o] = both.astype(jnp.bfloat16)
+
+    prepare(1)
+    pl.semaphore_wait(barrier, CHIPS + PLANES - 1)
+    halves.start()
     for o in reach:
         regroup(o, 0).start()
-
-    for o in order:
-        halves[o].wait_recv()
+    prepare(0)
+
+    halves.wait_recv()
+    for o in (2, 1, 3, 0):
         sel[0, o] = (sel[0, o].astype(jnp.float32) + core_in[o].astype(jnp.float32)).astype(jnp.bfloat16)
         if o != 0:
             picks[o].start()
@@ -233,12 +237,13 @@
             cores(y, o).start()
 
     def receivers(y):
-        for k in range(segs):
-            wf[y, k] = (whs[z, k] if type(y) is int else rcv[y, k]).astype(jnp.float32)
+        for side in range(2):
+            for o in range(CHIPS):
+                wf[y, side, o] = (whs[z, side, o] if type(y) is int else rcv[y, side, o]).astype(jnp.float32)
 
     def await_receivers(y):
         for h in range(2):
-            at = rcv.at[y, pl.ds(h * half, half)]
+            at = rcv.at[y, 1 - h]
             pltpu.make_async_remote_copy(
                 src_ref=at, dst_ref=at, send_sem=a_s.at[y, h], recv_sem=a_r.at[y, h],
                 device_id={"seg": seg_at(1)}, device_id_type=MESH).wait_recv()
@@ -248,17 +253,16 @@
         if s == 1:
             for o in range(CHIPS):
                 cores(y, o).wait_recv()
-        side = core if s == 0 else 1 - core
         ks = []
         for o in range(CHIPS):
             vf[o] = src[s, y, o].astype(jnp.float32)
-            ks.append(chip_at(CHIPS - o) * 2 + side)
+            ks.append((CHIPS - o) % CHIPS)
 
         def tile(t, carry):
             f = pl.ds(pl.multiple_of(t * 128, 128), 128)
             g = pl.ds(pl.multiple_of(freqs + t * 128, 128), 128)
-            cs = [wf[y, k, 0:own, f] for k in ks]
-            es = [wf[y, k, own:2 * own, f] for k in ks]
+            cs = [wf[y, s, k, 0:own, f] for k in ks]
+            es = [wf[y, s, k, own:2 * own, f] for k in ks]
             for r in range(own):
                 c = [jnp.broadcast_to(v[r:r + 1], (8, 128)) for v in cs]
                 e = [jnp.broadcast_to(v[r:r + 1], (8, 128)) for v in es]
@@ -279,8 +283,8 @@
 
     spread(0)
     receivers(0)
+    spread_far(y1)
     share(0)
-    spread_far(y1)
     spread_far(y2)
     for o in reach:
         regroup(o, 1).start()
@@ -311,7 +315,7 @@
     for r in range(own):
         out[:, r, :] = result[r * n_src:(r + 1) * n_src]
 
-    for copy in (*halves, *picks.values(), *(regroup(o, h) for o in range(1, PLANES) for h in range(2))):
+    for copy in (halves, *picks.values(), *(regroup(o, h) for o in range(1, PLANES) for h in range(2))):
         copy.wait_send()
     for y in range(PLANES):
         relay(y, lambda copy: copy.wait_send())
@@ -337,19 +341,19 @@
         ],
         out_specs=pl.BlockSpec(memory_space=pltpu.VMEM),
         scratch_shapes=[
-            pltpu.VMEM((2, segs, rows, freqs), bf16),
-            pltpu.VMEM((PLANES, segs, 2 * own, freqs), bf16),
+            pltpu.VMEM((2, CHIPS, 2, rows, freqs), bf16),
+            pltpu.VMEM((PLANES, 2, CHIPS, 2 * own, freqs), bf16),
             pltpu.VMEM((2, CHIPS, 2, n_src, freqs), bf16),
             pltpu.VMEM((CHIPS, 2, n_src, freqs), bf16),
             pltpu.VMEM((CHIPS, 2, n_src, freqs), bf16),
-            pltpu.VMEM((PLANES, segs, 2 * own, freqs), bf16),
+            pltpu.VMEM((PLANES, 2, CHIPS, 2 * own, freqs), bf16),
             pltpu.VMEM((2, PLANES, CHIPS, 2, n_src, freqs), bf16),
             pltpu.VMEM((CHIPS, 2, n_src, freqs), f32),
-            pltpu.VMEM((PLANES, segs, 2 * own, freqs), f32),
+            pltpu.VMEM((PLANES, 2, CHIPS, 2 * own, freqs), f32),
             pltpu.VMEM((own, n_src, 2 * freqs), f32),
             pltpu.VMEM((2, 2 * freqs, 2 * LAGS), bf16),
-            dma,
-            dma((CHIPS,)), dma((CHIPS,)),
+            dma((2, CHIPS)),
+            dma, dma,
             dma((CHIPS,)), dma((CHIPS,)),
             dma((PLANES, 2)), dma((PLANES, 2)),
             dma((2, PLANES)), dma((PLANES,)),
@@ -358,7 +362,7 @@
             dma,
         ],
         compiler_params=pltpu.CompilerParams(
-            collective_id=0, has_side_effects=True, vmem_limit_bytes=40 * 1024 * 1024),
+            collective_id=0, has_side_effects=True, vmem_limit_bytes=60 * 1024 * 1024),
     )(spectra, sources.T, jnp.asarray(lag_halves(freqs, LAGS)))
 
 

time: 37.6 us -> 38.4 us (1.021)
  Pallas kernels: 33.2 us -> 36.3 us
  local copies, waits for them, and re-layouts: 4.11 us -> 1.87 us
    pallas_call x1, Pallas kernels: 33.2 us -> 36.3 us  [fused(): pl.pallas_call(kernel, out_shape=jax.ShapeDtypeStruct((n_src, own, 2 * LA...]
    unnamed x7 -> x1, local copies, waits for them, and re-layouts: 4.11 us -> 1.87 us
where the time goes in v4:
time: 38.4 us; the launch traced here: 38.2 us
  Pallas kernels  36.3 us (95%)
  local copies, waits for them, and re-layouts  1.87 us (5%)
    pallas_call x1, Pallas kernels, fused(): pl.pallas_call(kernel, out_shape=jax.ShapeDtypeStruct((n_src, own, 2 * LA...  36.3 us
    unnamed x1, local copies, waits for them, and re-layouts  1.87 us

profile of v4, /device:TPU:0, one launch (start us, length us, event | category | flops | bytes accessed | tf_op | source)
XLA Modules:
  0.0 38.2 jit_solution(8504018323787768001)
XLA Ops:
  0.0 36.3 %shard_map.37 = f32[32,8,512]{2,1,0:T(8,128)} custom-call(bf16[2,8,32,512]{3,2,1,0:T(8,128)(2,1)} %spectra.1, s32[4,8]{1,0:T(4,128)} %bitcast.1, bf16[2,1024,512]{2,1,0:T(8,128)(2,1)} %constant.2.clone.table), custom_call_target="tpu_custom_call" | custom-call | tf_op jit(solution)/shard_map/pallas_call | solution.py:334
  36.3 1.9 %copy.5 = f32[32,8,512]{2,1,0:T(8,128)} copy(f32[32,8,512]{2,1,0:T(8,128)} %shard_map.37) | data formatting | bytes 1048576

commit v5 on v4

--- a/solution.py
+++ b/solution.py
@@ -113,7 +113,6 @@
         for o in range(CHIPS):
             segment(side, o).start()
     table_in = pltpu.make_async_copy(table, tab, t_sem)
-    table_in.start()
 
     def seg_at(o):
         return lax.rem(z + o, PLANES)
@@ -204,6 +203,7 @@
     prepare(1)
     pl.semaphore_wait(barrier, CHIPS + PLANES - 1)
     halves.start()
+    table_in.start()
     for o in reach:
         regroup(o, 0).start()
     prepare(0)
@@ -282,23 +282,34 @@
         lax.fori_loop(0, tiles, tile, 0)
 
     spread(0)
-    receivers(0)
     spread_far(y1)
+    spread_far(y2)
     share(0)
-    spread_far(y2)
     for o in reach:
         regroup(o, 1).start()
-    add(0, 0, True)
+    receivers(0)
+
+    at_end = first + last
+
+    @pl.when(at_end == 1)
+    def _():
+        add(0, 0, True)
+
     spread_far(y3)
+
+    @pl.when(at_end == 0)
+    def _():
+        add(0, 0, True)
+
+    share(y1)
     add(0, 1)
-    share(y1)
+    share(y2)
     await_receivers(y1)
     add(y1, 0)
-    share(y2)
     add(y1, 1)
+    share(y3)
     await_receivers(y2)
     add(y2, 0)
-    share(y3)
     add(y2, 1)
     await_receivers(y3)
     add(y3, 0)

time: 38.4 us -> 37.4 us (0.974)
  Pallas kernels: 36.3 us -> 35.3 us
    pallas_call x1, Pallas kernels: 36.3 us -> 35.3 us  [fused(): pl.pallas_call(kernel, out_shape=jax.ShapeDtypeStruct((n_src, own, 2 * LA...]
where the time goes in v5:
time: 37.4 us; the launch traced here: 37.2 us
  Pallas kernels  35.3 us (94%)
  local copies, waits for them, and re-layouts  1.87 us (5%)
    pallas_call x1, Pallas kernels, fused(): pl.pallas_call(kernel, out_shape=jax.ShapeDtypeStruct((n_src, own, 2 * LA...  35.3 us
    unnamed x1, local copies, waits for them, and re-layouts  1.87 us

profile of v5, /device:TPU:0, one launch (start us, length us, event | category | flops | bytes accessed | tf_op | source)
XLA Modules:
  0.0 37.2 jit_solution(7604073630493097024)
XLA Ops:
  0.0 35.3 %shard_map.37 = f32[32,8,512]{2,1,0:T(8,128)} custom-call(bf16[2,8,32,512]{3,2,1,0:T(8,128)(2,1)} %spectra.1, s32[4,8]{1,0:T(4,128)} %bitcast.1, bf16[2,1024,512]{2,1,0:T(8,128)(2,1)} %constant.2.clone.table), custom_call_target="tpu_custom_call" | custom-call | tf_op jit(solution)/shard_map/pallas_call | solution.py:345
  35.3 1.9 %copy.5 = f32[32,8,512]{2,1,0:T(8,128)} copy(f32[32,8,512]{2,1,0:T(8,128)} %shard_map.37) | data formatting | bytes 1048576

commit v6 on v5

--- a/solution.py
+++ b/solution.py
@@ -285,20 +285,22 @@
     spread_far(y1)
     spread_far(y2)
     share(0)
-    for o in reach:
-        regroup(o, 1).start()
     receivers(0)
 
     at_end = first + last
 
     @pl.when(at_end == 1)
     def _():
+        for o in reach:
+            regroup(o, 1).start()
         add(0, 0, True)
 
     spread_far(y3)
 
     @pl.when(at_end == 0)
     def _():
+        for o in reach:
+            regroup(o, 1).start()
         add(0, 0, True)
 
     share(y1)

time: 37.4 us -> 37 us (0.989)
  Pallas kernels: 35.3 us -> 34.8 us
    pallas_call x1, Pallas kernels: 35.3 us -> 34.8 us  [fused(): pl.pallas_call(kernel, out_shape=jax.ShapeDtypeStruct((n_src, own, 2 * LA...]
where the time goes in v6:
time: 37 us; the launch traced here: 36.7 us
  Pallas kernels  34.8 us (94%)
  local copies, waits for them, and re-layouts  1.87 us (5%)
    pallas_call x1, Pallas kernels, fused(): pl.pallas_call(kernel, out_shape=jax.ShapeDtypeStruct((n_src, own, 2 * LA...  34.8 us
    unnamed x1, local copies, waits for them, and re-layouts  1.87 us

profile of v6, /device:TPU:0, one launch (start us, length us, event | category | flops | bytes accessed | tf_op | source)
XLA Modules:
  0.0 36.7 jit_solution(15973531604779857655)
XLA Ops:
  0.0 34.8 %shard_map.37 = f32[32,8,512]{2,1,0:T(8,128)} custom-call(bf16[2,8,32,512]{3,2,1,0:T(8,128)(2,1)} %spectra.1, s32[4,8]{1,0:T(4,128)} %bitcast.1, bf16[2,1024,512]{2,1,0:T(8,128)(2,1)} %constant.2.clone.table), custom_call_target="tpu_custom_call" | custom-call | tf_op jit(solution)/shard_map/pallas_call | solution.py:347
  34.9 1.9 %copy.5 = f32[32,8,512]{2,1,0:T(8,128)} copy(f32[32,8,512]{2,1,0:T(8,128)} %shard_map.37) | data formatting | bytes 1048576
